TPU v7x, 32 devices: a whole 2x2x4 slice. The times are simulated.
32 devices in a mesh: dp: 8 (over z, core), ctx: 4 (over y, x).
Axes of the slice: x: 2, y: 2, z: 4, core: 2. Of those that a mesh axis runs over, the one named last changes fastest.
Arguments:
- q_rows: bfloat16 [16384, 2048], P(('dp', 'ctx')), may hold values from -8 to 8
- kv_rows: bfloat16 [16384, 1024], P(('dp', 'ctx')), may hold values from -8 to 8
- packed_slot: int32 [16384], P(('dp', 'ctx')), may hold values from 0 to 16383, as said below
- doc_ids: int32 [8, 2048], P('dp', 'ctx'), may hold values from 0 to 5, never falling along the last dimension, each value on 1 to 1024 neighbouring positions
Outputs:
- attended: bfloat16 [16384, 2048], P(('dp', 'ctx'))
Inputs may be any that keep to these rules, and one draw needn't show every extreme that they name: `packed_slot`: A permutation of the packed positions; the 512 loader rows of every device send exactly 16 rows to the packed positions of each device, position p lying on device p // 512 in the order of dp+ctx. `doc_ids`: document numbers never fall along a sequence; a document has 1 to 1024 positions.
All inputs are finite; a program needn't handle non-finite values.
Results may differ from a plain program's by a relative error of at most 0.0038.
Values may be sent and summed in bfloat16 or wider, within the bound.
No kernel may reach another device: no remote copies, remote signals or barrier semaphores. Data moves between devices by JAX's collectives and lax.ppermute only.
A program may use at most 192 MiB of HBM per device.

v0:
```python
import functools
import math

import jax
import jax.numpy as jnp
from jax import lax
from jax.experimental import pallas as pl
from jax.experimental.pallas import tpu as pltpu
from jax.sharding import PartitionSpec as P

HEADS = 16
KV_HEADS = 4
HD = 128
GROUP = 4
KV_COLS = 2 * KV_HEADS * HD
GROUP_COLS = GROUP * HD
META = 128
STEP = 256
NEG = -1e30
MIB = 1 << 20

F32 = jnp.float32
BF16 = jnp.bfloat16


def dot(a, b):
    return jnp.dot(a, b, preferred_element_type=F32)


def dot_nt(a, b):
    return lax.dot_general(a, b, (((1,), (1,)), ((), ())), preferred_element_type=F32)


def iota(shape, dim):
    return lax.broadcasted_iota(jnp.int32, shape, dim)


def send_matrix(slot, devices):
    rows = slot.shape[1]
    target = slot // rows
    one_hot = (iota((devices, rows), 0) == target).astype(F32)
    before = (iota((rows, rows), 0) < iota((rows, rows), 1)).astype(BF16)
    rank = jnp.sum(dot(one_hot.astype(BF16), before) * one_hot, axis=0, keepdims=True)
    where_to = target * (rows // devices) + rank.astype(jnp.int32)
    return (iota((rows, rows), 0) == where_to).astype(BF16)


def pack_kv_kernel(devices, slot_ref, kv_hbm, out_ref, kv_ref, sem):
    copy = pltpu.make_async_copy(kv_hbm, kv_ref, sem)
    copy.start()
    slot = slot_ref[...]
    rows = slot.shape[1]
    matrix = send_matrix(slot, devices)
    local = slot % rows
    which = iota((META, rows), 0)
    digits = jnp.where(which == 0, local // 16, jnp.where(which == 1, local % 16, 0))
    out_ref[:, KV_COLS:] = dot_nt(matrix, digits.astype(BF16)).astype(BF16)
    copy.wait()
    out_ref[:, :KV_COLS] = dot(matrix, kv_ref[...]).astype(BF16)


def pack_q_kernel(devices, slot_ref, q_ref, out_ref, matrix_ref):
    @pl.when(pl.program_id(0) == 0)
    def _():
        matrix_ref[...] = send_matrix(slot_ref[...], devices)

    out_ref[...] = dot(matrix_ref[...], q_ref[...]).astype(BF16)


def sort_kv_kernel(got_ref, place_ref, kv_ref, *piece_refs):
    rows = got_ref.shape[0]
    half = KV_HEADS * HD
    pick = (iota((8, META), 0) == iota((8, META), 1)).astype(BF16)
    digits = dot_nt(pick, got_ref[:, KV_COLS:])
    place = (digits[0:1] * 16 + digits[1:2]).astype(jnp.int32)
    place_ref[...] = place
    matrix = (iota((rows, rows), 0) == place).astype(BF16)
    kv_ref[:rows, :] = dot(matrix, got_ref[:, :half]).astype(BF16)
    kv_ref[rows:, :] = dot(matrix, got_ref[:, half:KV_COLS]).astype(BF16).T
    at = 0
    for piece_ref in piece_refs:
        piece_ref[...] = kv_ref[at : at + piece_ref.shape[0], :]
        at += piece_ref.shape[0]


def attend_kernel(sources, early_ref, place_ref, start_ref, q_ref, *refs):
    kv_refs = refs[:-7]
    out_ref, matrix_ref, bias_ref, q_buf, key_buf, value_buf, score_buf = refs[-7:]
    rows = q_ref.shape[0]
    width = key_buf.shape[0]
    begin = width - rows
    scale = math.log2(math.e) / math.sqrt(HD)
    first, early_steps, all_early = early_ref[0], early_ref[1], early_ref[2]

    @pl.when(pl.program_id(0) == 0)
    def _():
        matrix_ref[...] = (iota((rows, rows), 0) == place_ref[...]).astype(BF16)
        key, query = iota((rows, rows), 0), iota((rows, rows), 1)
        allowed = (key + begin >= start_ref[...]) & (key <= query)
        bias_ref[...] = jnp.where(allowed, 0.0, NEG)
        value_buf[HD:, :] = jnp.ones((value_buf.shape[0] - HD, width), BF16)

    q_buf[...] = dot(matrix_ref[...], q_ref[...]).astype(BF16)
    group, at = pl.program_id(0), 0
    for b, block in enumerate(sources):
        keys, values = [], []
        for count in block:
            refs_here = kv_refs[at : at + count]
            at += count
            if count == 2:
                key, value = (ref[...] for ref in refs_here)
            else:
                key = jnp.concatenate([ref[...] for ref in refs_here[:2]], axis=0)
                value = jnp.where(group < KV_HEADS // 2, refs_here[2][...], refs_here[3][...])
            keys.append(key)
            values.append(value)
        here = slice(b * rows, (b + 1) * rows)
        key_buf[here, :] = sum(keys[1:], keys[0])
        value_buf[:HD, here] = sum(values[1:], values[0])

    def run(counts):
        def steps_of(tile):
            return list(range(begin - counts[tile] * STEP, begin + (tile + 1) * STEP, STEP))

        def queries_of(tile):
            return slice(tile * STEP, (tile + 1) * STEP)

        def score(slot, tile, h, i, at, tops):
            part = dot_nt(
                key_buf[at : at + STEP, :], q_buf[queries_of(tile), h * HD : (h + 1) * HD]
            )
            own = at >= begin
            if own:
                part = part + bias_ref[at - begin : at - begin + STEP, queries_of(tile)]
            elif i == 0:
                part = jnp.where(iota((STEP, 1), 0) + at >= first, part, NEG)
            score_buf[slot, i * STEP : (i + 1) * STEP, :] = part
            peak = jnp.max(part.reshape(STEP // 8, 8, STEP), axis=0)
            tops[own] = jnp.maximum(tops[own], peak) if own in tops else peak

        def largest_of(tile, tops):
            own = jnp.max(tops[True], axis=0, keepdims=True)
            if False not in tops:
                return {True: own}
            shared = jnp.where(start_ref[:, queries_of(tile)] == first, 0.0, -NEG)
            early = jnp.max(tops[False], axis=0, keepdims=True)
            both = jnp.maximum(own, early - shared)
            return {True: both, False: both + shared}

        def weigh(slot, i, at, largest, summed):
            part = score_buf[slot, i * STEP : (i + 1) * STEP, :]
            probs = jnp.exp2((part - largest[at >= begin]) * scale).astype(BF16)
            added = dot(value_buf[:, at : at + STEP], probs)
            return added if summed is None else summed + added

        def finish(tile, h, summed):
            result = (summed[:HD] * (1.0 / summed[HD : HD + 1])).astype(BF16)
            out_ref[queries_of(tile), h * HD : (h + 1) * HD] = result.T

        chains = [(tile, h) for tile in range(rows // STEP) for h in range(GROUP)]
        largest = {}
        for c in range(len(chains) + 1):
            tops, summed = {}, None
            now = steps_of(chains[c][0]) if c < len(chains) else []
            past = steps_of(chains[c - 1][0]) if c else []
            for i in range(max(len(now), len(past))):
                if i < len(now):
                    score(c % 2, *chains[c], i, now[i], tops)
                if i < len(past):
                    summed = weigh((c - 1) % 2, i, past[i], largest[c - 1], summed)
            if now:
                largest[c] = largest_of(chains[c][0], tops)
            if past:
                finish(*chains[c - 1], summed)

    tiles = rows // STEP
    for early in range(begin // STEP + 1):
        for whole in (False, True) if early else (True,):
            counts = [early if whole or t == 0 else 0 for t in range(tiles)]
            pl.when((early_steps == early) & (all_early == int(whole)))(functools.partial(run, counts))


def all_to_all(x):
    return lax.all_to_all(x, ("dp", "ctx"), split_axis=0, concat_axis=0, tiled=True)


def attend(early, place, start, q_got, kv):
    rows = q_got.shape[0]
    blocks = len(kv)
    width = blocks * rows
    keys_of = pl.BlockSpec((rows, HD), lambda g, *_: (0, g))
    values_of = pl.BlockSpec((HD, rows), lambda g, *_: (rows // HD + g, 0))
    keys_of_half = pl.BlockSpec((rows // 2, HD), lambda g, *_: (0, g))
    values_of_half = pl.BlockSpec((HD, rows), lambda g, *_: (g % (KV_HEADS // 2), 0))
    arrays, specs = [], []
    for block in kv:
        for source in block:
            one = len(source) == 1
            arrays += list(source) * 2 if one else list(source)
            specs += [keys_of, values_of] if one else [keys_of_half] * 2 + [values_of_half] * 2
    sources = [[2 if len(source) == 1 else 4 for source in block] for block in kv]
    whole = lambda shape: pl.BlockSpec(shape, lambda g, *_: (0, 0))
    return pl.pallas_call(
        functools.partial(attend_kernel, sources),
        out_shape=jax.ShapeDtypeStruct(q_got.shape, BF16),
        grid_spec=pltpu.PrefetchScalarGridSpec(
            num_scalar_prefetch=1,
            grid=(KV_HEADS,),
            in_specs=[whole((1, rows)), whole((1, rows))]
            + [pl.BlockSpec((rows, GROUP_COLS), lambda g, *_: (0, g))]
            + specs,
            out_specs=pl.BlockSpec((rows, GROUP_COLS), lambda g, *_: (0, g)),
            scratch_shapes=[
                pltpu.VMEM((rows, rows), BF16),
                pltpu.VMEM((rows, rows), F32),
                pltpu.VMEM((rows, GROUP_COLS), BF16),
                pltpu.VMEM((width, HD), BF16),
                pltpu.VMEM((HD + 16, width), BF16),
                pltpu.VMEM((2, width, STEP), F32),
            ],
        ),
        compiler_params=pltpu.CompilerParams(vmem_limit_bytes=62 * MIB),
        name="attend",
    )(early, place, start, q_got, *arrays)


def per_device(q_rows, kv_rows, packed_slot, doc_ids):
    rows = q_rows.shape[0]
    ctx_size = lax.axis_size("ctx")
    devices = lax.axis_size("dp") * ctx_size
    pack = rows * ctx_size
    doc_max = pack // 2
    before = min(ctx_size - 1, -(-(doc_max - 1) // rows))
    blocks = before + 1
    slot = packed_slot.reshape(1, rows)
    params = pltpu.CompilerParams(vmem_limit_bytes=48 * MIB)

    kv_out = pl.pallas_call(
        functools.partial(pack_kv_kernel, devices),
        out_shape=jax.ShapeDtypeStruct((rows, KV_COLS + META), BF16),
        in_specs=[pl.BlockSpec(memory_space=pltpu.VMEM), pl.BlockSpec(memory_space=pl.ANY)],
        scratch_shapes=[pltpu.VMEM(kv_rows.shape, BF16), pltpu.SemaphoreType.DMA],
        compiler_params=pltpu.CompilerParams(vmem_limit_bytes=60 * MIB),
        name="pack_kv",
    )(slot, kv_rows)

    def from_before(x, distance):
        return lax.ppermute(x, "ctx", [(i, i + distance) for i in range(ctx_size - distance)])

    kv_out, docs = lax.optimization_barrier((kv_out, doc_ids.reshape(rows) + 1))
    kv_got = all_to_all(kv_out)

    doc_line = jnp.concatenate([from_before(docs, d) for d in range(before, 0, -1)] + [docs])
    start = jnp.sum((doc_line[None, :] < docs[:, None]).astype(jnp.int32), axis=1)
    begin = before * rows
    first = start[0]
    early_steps = jnp.maximum(begin - first + STEP - 1, 0) // STEP
    all_early = (start[rows - STEP] == first) | (early_steps == 0)
    early = jnp.stack([first, early_steps, all_early.astype(jnp.int32)])
    q_rows, early, start = lax.optimization_barrier((q_rows, early, start.reshape(1, rows)))

    q_out = pl.pallas_call(
        functools.partial(pack_q_kernel, devices),
        out_shape=jax.ShapeDtypeStruct(q_rows.shape, BF16),
        grid=(KV_HEADS,),
        in_specs=[
            pl.BlockSpec((1, rows), lambda g: (0, 0)),
            pl.BlockSpec((rows, GROUP_COLS), lambda g: (0, g)),
        ],
        out_specs=pl.BlockSpec((rows, GROUP_COLS), lambda g: (0, g)),
        scratch_shapes=[pltpu.VMEM((rows, rows), BF16)],
        compiler_params=params,
        name="pack_q",
    )(slot, q_rows)
    q_got = all_to_all(q_out)

    relay = ctx_size == 4 and before == 2
    pieces = (rows // 2, rows // 2, KV_HEADS // 2 * HD, KV_HEADS // 2 * HD) if relay else ()
    place, kv_here, *pieces = pl.pallas_call(
        sort_kv_kernel,
        out_shape=[jax.ShapeDtypeStruct((1, rows), jnp.int32)]
        + [jax.ShapeDtypeStruct((n, rows), BF16) for n in (rows + KV_HEADS * HD, *pieces)],
        compiler_params=params,
        name="sort_kv",
    )(kv_got)

    if relay:
        far = [lax.ppermute(x, "ctx", [(0, 2), (1, 3)]) for x in pieces]
        near = lax.ppermute(kv_here, "ctx", [(0, 1), (2, 3)])
        hop = [lax.ppermute(x, "ctx", [(3, 2)]) for x in far]
        kv = [[far], [[near], hop], [[kv_here]]]
    else:
        kv = [[[from_before(kv_here, d)]] for d in range(before, 0, -1)] + [[[kv_here]]]
    return attend(early, place, start, q_got, kv)


def solution(mesh):
    return jax.shard_map(
        per_device,
        mesh=mesh,
        in_specs=(P(("dp", "ctx"), None), P(("dp", "ctx"), None), P(("dp", "ctx")), P("dp", "ctx")),
        out_specs=P(("dp", "ctx"), None),
        check_vma=False,
    )
```

profile of v0, /device:TPU:5, one launch (start us, length us, event | category | flops | bytes accessed | tf_op | source)
XLA Modules:
  0.0 118.8 jit_solution(15160258407115885902)
XLA Ops:
  0.0 0.7 broadcast_add_fusion
  0.7 0.0 copy-start.1
  0.7 0.0 copy-start.2
  0.7 3.8 %pack_kv.1 = bf16[512,1152]{1,0:T(8,128)(2,1)} custom-call(s32[1,512]{1,0:T(1,128)} %bitcast.13, bf16[512,1024]{1,0:T(8,128)(2,1)} %kv_hbm.1), custom_call_target="tpu_custom_call" | custom-call | tf_op jit(solution)/shard_map/pack_kv/pallas_call | solution.py:238
  4.5 6.4 %all-to-all-start = ((bf16[32,16,1152]{2,1,0:T(8,128)(2,1)}), bf16[32,16,1152]{2,1,0:T(8,128)(2,1)S(1)}, u32[]{:S(2)}, u32[]{:S(2)}) async-start(bf16[32,16,1152]{2,1,0:T(8,128)(2,1)} %bitcast.15), calls=%async_computation | async-start | bytes 2359296 | tf_op jit(solution)/shard_map/all_to_all | solution.py:184
  10.9 1.3 %collective-permute-start = (s32[512]{0:T(512)S(1)}, s32[512]{0:T(512)S(1)}, u32[]{:S(2)}, u32[]{:S(2)}) collective-permute-start(s32[512]{0:T(512)S(1)} %bitcast.16), channel_id=1, source_target_pairs={{0,2},{1,3},{4,6},{5,7},{8,10},{9,11},{12,14},{13,15},{16,18},{17,... | collective-permute-start | bytes 6152 | tf_op jit(solution)/shard_map/ppermute | solution.py:248
  12.2 3.1 %collective-permute-start.1 = (s32[512]{0:T(512)S(1)}, s32[512]{0:T(512)S(1)}, u32[]{:S(2)}, u32[]{:S(2)}) collective-permute-start(s32[512]{0:T(512)S(1)} %bitcast.17), channel_id=1, source_target_pairs={{0,1},{1,2},{2,3},{4,5},{5,6},{6,7},{8,9},{9,10},{10,11},{12,13},{... | collective-permute-start | bytes 6152 | tf_op jit(solution)/shard_map/ppermute | solution.py:248
  15.3 0.3 collective-permute-done
  15.7 2.7 %collective-permute-done.1 = s32[512]{0:T(512)S(1)} collective-permute-done((s32[512]{0:T(512)S(1)}, s32[512]{0:T(512)S(1)}, u32[]{:S(2)}, u32[]{:S(2)}) %collective-permute-start.1) | collective-permute-done | bytes 2080 | tf_op jit(solution)/shard_map/ppermute | solution.py:248
  18.4 0.5 convert_reduce_fusion
  18.9 0.0 copy-start.12
  18.9 0.5 fusion
  21.4 1.3 %pad_add_fusion.1.early_ref = s32[3]{0:T(128)} fusion(s32[1]{0:T(128)} %bitcast.6, s32[1]{0:T(128)} %bitcast.4, s32[1]{0:T(128)} %get-tuple-element.27), kind=kLoop, calls=%fused_computation.3 | loop fusion | flops 6 | bytes 24 | tf_op jit(solution)/shard_map/stack | solution.py:259
  22.6 0.0 copy-done.1
  22.6 0.0 copy-done.2
  22.6 3.5 %pack_q.1 = bf16[512,2048]{1,0:T(8,128)(2,1)} custom-call(s32[1,512]{1,0:T(1,128)S(1)} %bitcast.14, bf16[512,2048]{1,0:T(8,128)(2,1)S(1)} %copy-done.1), custom_call_target="tpu_custom_call" | custom-call | tf_op jit(solution)/shard_map/pack_q/pallas_call | solution.py:262
  26.1 0.0 copy-done.12
  26.1 13.8 %all-to-all-done = bf16[32,16,1152]{2,1,0:T(8,128)(2,1)S(1)} async-done(((bf16[32,16,1152]{2,1,0:T(8,128)(2,1)}), bf16[32,16,1152]{2,1,0:T(8,128)(2,1)S(1)}, u32[]{:S(2)}, u32[]{:S(2)}) %all-to-all-start) | async-done | bytes 1179680 | tf_op jit(solution)/shard_map/all_to_all | solution.py:184
  39.9 3.8 %all-to-all-start.1 = ((bf16[32,16,2048]{2,1,0:T(8,128)(2,1)}), bf16[32,16,2048]{2,1,0:T(8,128)(2,1)}, u32[]{:S(2)}, u32[]{:S(2)}) async-start(bf16[32,16,2048]{2,1,0:T(8,128)(2,1)} %bitcast.10), calls=%async_computation.1 | async-start | bytes 4194304 | tf_op jit(solution)/shard_map/all_to_all | solution.py:184
  43.7 0.9 sort_kv.1
  44.6 0.0 copy-start.3
  44.6 0.0 copy-start
  44.6 4.1 %collective-permute-start.6 = (bf16[1024,512]{1,0:T(8,128)(2,1)S(1)}, bf16[1024,512]{1,0:T(8,128)(2,1)}, u32[]{:S(2)}, u32[]{:S(2)}) collective-permute-start(bf16[1024,512]{1,0:T(8,128)(2,1)S(1)} %get-tuple-element.26.refs_10_.refs_11_), channel_id=1, source_target_pairs={{0,1},{2,3},{4,5},{6,7},{8,9},{10,11},{12,13},{14,15},{16,17},{18,... | collective-permute-start | bytes 3145736 | tf_op jit(solution)/shard_map/ppermute | solution.py:289
  48.7 1.3 %collective-permute-start.5 = (bf16[256,512]{1,0:T(8,128)(2,1)S(1)}, bf16[256,512]{1,0:T(8,128)(2,1)S(1)}, u32[]{:S(2)}, u32[]{:S(2)}) collective-permute-start(bf16[256,512]{1,0:T(8,128)(2,1)S(1)} %get-tuple-element.25), channel_id=1, source_target_pairs={{0,2},{1,3},{4,6},{5,7},{8,10},{9,11},{12,14},{13,15},{16,18},{17,... | collective-permute-start | bytes 786440 | tf_op jit(solution)/shard_map/ppermute | solution.py:288
  50.0 1.3 %collective-permute-start.2 = (bf16[256,512]{1,0:T(8,128)(2,1)S(1)}, bf16[256,512]{1,0:T(8,128)(2,1)S(1)}, u32[]{:S(2)}, u32[]{:S(2)}) collective-permute-start(bf16[256,512]{1,0:T(8,128)(2,1)S(1)} %get-tuple-element.22), channel_id=1, source_target_pairs={{0,2},{1,3},{4,6},{5,7},{8,10},{9,11},{12,14},{13,15},{16,18},{17,... | collective-permute-start | bytes 786440 | tf_op jit(solution)/shard_map/ppermute | solution.py:288
  51.3 1.3 %collective-permute-start.3 = (bf16[256,512]{1,0:T(8,128)(2,1)S(1)}, bf16[256,512]{1,0:T(8,128)(2,1)S(1)}, u32[]{:S(2)}, u32[]{:S(2)}) collective-permute-start(bf16[256,512]{1,0:T(8,128)(2,1)S(1)} %get-tuple-element.23), channel_id=1, source_target_pairs={{0,2},{1,3},{4,6},{5,7},{8,10},{9,11},{12,14},{13,15},{16,18},{17,... | collective-permute-start | bytes 786440 | tf_op jit(solution)/shard_map/ppermute | solution.py:288
  52.6 1.3 %collective-permute-start.4 = (bf16[256,512]{1,0:T(8,128)(2,1)S(1)}, bf16[256,512]{1,0:T(8,128)(2,1)S(1)}, u32[]{:S(2)}, u32[]{:S(2)}) collective-permute-start(bf16[256,512]{1,0:T(8,128)(2,1)S(1)} %get-tuple-element.24), channel_id=1, source_target_pairs={{0,2},{1,3},{4,6},{5,7},{8,10},{9,11},{12,14},{13,15},{16,18},{17,... | collective-permute-start | bytes 786440 | tf_op jit(solution)/shard_map/ppermute | solution.py:288
  53.9 10.2 %collective-permute-done.5.refs_3_ = bf16[256,512]{1,0:T(8,128)(2,1)S(1)} collective-permute-done((bf16[256,512]{1,0:T(8,128)(2,1)S(1)}, bf16[256,512]{1,0:T(8,128)(2,1)S(1)}, u32[]{:S(2)}, u32[]{:S(2)}) %collective-permute-start.5) | collective-permute-done | bytes 262176 | tf_op jit(solution)/shard_map/ppermute | solution.py:288
  64.1 0.0 copy-start.4
  64.1 1.3 %collective-permute-start.10 = (bf16[256,512]{1,0:T(8,128)(2,1)S(1)}, bf16[256,512]{1,0:T(8,128)(2,1)S(1)}, u32[]{:S(2)}, u32[]{:S(2)}) collective-permute-start(bf16[256,512]{1,0:T(8,128)(2,1)S(1)} %collective-permute-done.5.refs_3_), channel_id=1, source_target_pairs={{3,2},{7,6},{11,10},{15,14},{19,18},{23,22},{27,26},{31,30}} | collective-permute-start | bytes 786440 | tf_op jit(solution)/shard_map/ppermute | solution.py:290
  65.4 9.3 %collective-permute-done.2.refs_0_ = bf16[256,512]{1,0:T(8,128)(2,1)S(1)} collective-permute-done((bf16[256,512]{1,0:T(8,128)(2,1)S(1)}, bf16[256,512]{1,0:T(8,128)(2,1)S(1)}, u32[]{:S(2)}, u32[]{:S(2)}) %collective-permute-start.2) | collective-permute-done | bytes 262176 | tf_op jit(solution)/shard_map/ppermute | solution.py:288
  74.7 0.0 copy-start.5
  74.7 1.3 %collective-permute-start.7 = (bf16[256,512]{1,0:T(8,128)(2,1)S(1)}, bf16[256,512]{1,0:T(8,128)(2,1)S(1)}, u32[]{:S(2)}, u32[]{:S(2)}) collective-permute-start(bf16[256,512]{1,0:T(8,128)(2,1)S(1)} %collective-permute-done.2.refs_0_), channel_id=1, source_target_pairs={{3,2},{7,6},{11,10},{15,14},{19,18},{23,22},{27,26},{31,30}} | collective-permute-start | bytes 786440 | tf_op jit(solution)/shard_map/ppermute | solution.py:290
  76.0 5.1 %collective-permute-done.3.refs_1_ = bf16[256,512]{1,0:T(8,128)(2,1)S(1)} collective-permute-done((bf16[256,512]{1,0:T(8,128)(2,1)S(1)}, bf16[256,512]{1,0:T(8,128)(2,1)S(1)}, u32[]{:S(2)}, u32[]{:S(2)}) %collective-permute-start.3) | collective-permute-done | bytes 262176 | tf_op jit(solution)/shard_map/ppermute | solution.py:288
  81.1 0.0 copy-start.6
  81.1 1.3 %collective-permute-start.8 = (bf16[256,512]{1,0:T(8,128)(2,1)S(1)}, bf16[256,512]{1,0:T(8,128)(2,1)S(1)}, u32[]{:S(2)}, u32[]{:S(2)}) collective-permute-start(bf16[256,512]{1,0:T(8,128)(2,1)S(1)} %collective-permute-done.3.refs_1_), channel_id=1, source_target_pairs={{3,2},{7,6},{11,10},{15,14},{19,18},{23,22},{27,26},{31,30}} | collective-permute-start | bytes 786440 | tf_op jit(solution)/shard_map/ppermute | solution.py:290
  82.4 6.3 %collective-permute-done.4.refs_2_ = bf16[256,512]{1,0:T(8,128)(2,1)S(1)} collective-permute-done((bf16[256,512]{1,0:T(8,128)(2,1)S(1)}, bf16[256,512]{1,0:T(8,128)(2,1)S(1)}, u32[]{:S(2)}, u32[]{:S(2)}) %collective-permute-start.4) | collective-permute-done | bytes 262176 | tf_op jit(solution)/shard_map/ppermute | solution.py:288
  88.7 0.0 copy-start.7
  88.7 1.3 %collective-permute-start.9 = (bf16[256,512]{1,0:T(8,128)(2,1)S(1)}, bf16[256,512]{1,0:T(8,128)(2,1)S(1)}, u32[]{:S(2)}, u32[]{:S(2)}) collective-permute-start(bf16[256,512]{1,0:T(8,128)(2,1)S(1)} %collective-permute-done.4.refs_2_), channel_id=1, source_target_pairs={{3,2},{7,6},{11,10},{15,14},{19,18},{23,22},{27,26},{31,30}} | collective-permute-start | bytes 786440 | tf_op jit(solution)/shard_map/ppermute | solution.py:290
  90.0 0.0 collective-permute-done.10.refs_9_
  90.0 0.0 copy-start.8
  90.0 0.0 collective-permute-done.7.refs_6_
  90.1 0.0 copy-start.9
  90.1 3.8 %collective-permute-done.8.refs_7_ = bf16[256,512]{1,0:T(8,128)(2,1)S(1)} collective-permute-done((bf16[256,512]{1,0:T(8,128)(2,1)S(1)}, bf16[256,512]{1,0:T(8,128)(2,1)S(1)}, u32[]{:S(2)}, u32[]{:S(2)}) %collective-permute-start.8) | collective-permute-done | bytes 262176 | tf_op jit(solution)/shard_map/ppermute | solution.py:290
  93.9 0.0 copy-done.7
  93.9 0.0 copy-start.10
  93.9 5.6 %collective-permute-done.9.refs_8_ = bf16[256,512]{1,0:T(8,128)(2,1)S(1)} collective-permute-done((bf16[256,512]{1,0:T(8,128)(2,1)S(1)}, bf16[256,512]{1,0:T(8,128)(2,1)S(1)}, u32[]{:S(2)}, u32[]{:S(2)}) %collective-permute-start.9) | collective-permute-done | bytes 262176 | tf_op jit(solution)/shard_map/ppermute | solution.py:290
  99.5 0.0 copy-done.8
  99.5 0.0 copy-done.9
  99.5 0.0 copy-done.10
  99.5 0.0 copy-start.11
  99.5 0.0 collective-permute-done.6.refs_4_.refs_5_
  99.5 0.0 copy-done.3
  99.5 0.0 all-to-all-done.1
  99.5 0.7 copy-done.11
  100.2 0.0 copy-done
  100.2 0.0 copy-done.4
  100.2 0.0 copy-done.5
  100.2 0.0 copy-done.6
  100.2 18.5 %attend.1 = bf16[512,2048]{1,0:T(8,128)(2,1)} custom-call(s32[3]{0:T(128)} %pad_add_fusion.1.early_ref, s32[1,512]{1,0:T(1,128)} %copy-done.3, s32[1,512]{1,0:T(1,128)} %bitcast.20, bf16[512,2048]{1,0:T(8,128)(2,1)} %bitcast.11.q_ref, bf16[256,512]{1,0:T(8,128)(2,1)} %copy-done.5, bf16[256,512]{1,0:T(8,128)(2,1)} %copy-done.6, bf16[256,512]{1,0:T(8,128)(2,1)} %copy-done.7, ...), custom_call_target="tpu_custom_call" | custom-call | tf_op jit(solution)/shard_map/attend/pallas_call | solution.py:203
  (1 shorter events, 0.0 us)
Async XLA Ops:
  0.7 21.9 %copy-start.1 = (bf16[512,2048]{1,0:T(8,128)(2,1)S(1)}, bf16[512,2048]{1,0:T(8,128)(2,1)}, u32[]{:S(2)}) copy-start(bf16[512,2048]{1,0:T(8,128)(2,1)} %q_ref) | copy-start | bytes 6291460
  0.7 21.9 %copy-start.2 = (s32[512]{0:T(512)S(1)}, s32[512]{0:T(512)}, u32[]{:S(2)}) copy-start(s32[512]{0:T(512)} %param.6) | copy-start | bytes 6148
  4.5 35.4 %all-to-all-start = ((bf16[32,16,1152]{2,1,0:T(8,128)(2,1)}), bf16[32,16,1152]{2,1,0:T(8,128)(2,1)S(1)}, u32[]{:S(2)}, u32[]{:S(2)}) async-start(bf16[32,16,1152]{2,1,0:T(8,128)(2,1)} %bitcast.15), calls=%async_computation | async-start | bytes 2359296 | tf_op jit(solution)/shard_map/all_to_all | solution.py:184
  10.9 4.7 %collective-permute-start = (s32[512]{0:T(512)S(1)}, s32[512]{0:T(512)S(1)}, u32[]{:S(2)}, u32[]{:S(2)}) collective-permute-start(s32[512]{0:T(512)S(1)} %bitcast.16), channel_id=1, source_target_pairs={{0,2},{1,3},{4,6},{5,7},{8,10},{9,11},{12,14},{13,15},{16,18},{17,... | collective-permute-start | bytes 6152 | tf_op jit(solution)/shard_map/ppermute | solution.py:248
  12.2 6.1 %collective-permute-start.1 = (s32[512]{0:T(512)S(1)}, s32[512]{0:T(512)S(1)}, u32[]{:S(2)}, u32[]{:S(2)}) collective-permute-start(s32[512]{0:T(512)S(1)} %bitcast.17), channel_id=1, source_target_pairs={{0,1},{1,2},{2,3},{4,5},{5,6},{6,7},{8,9},{9,10},{10,11},{12,13},{... | collective-permute-start | bytes 6152 | tf_op jit(solution)/shard_map/ppermute | solution.py:248
  18.9 7.2 %copy-start.12 = (s32[512]{0:T(512)}, s32[512]{0:T(512)S(1)}, u32[]{:S(2)}) copy-start(s32[512]{0:T(512)S(1)} %convert_reduce_fusion) | copy-start | bytes 6148
  39.9 59.6 %all-to-all-start.1 = ((bf16[32,16,2048]{2,1,0:T(8,128)(2,1)}), bf16[32,16,2048]{2,1,0:T(8,128)(2,1)}, u32[]{:S(2)}, u32[]{:S(2)}) async-start(bf16[32,16,2048]{2,1,0:T(8,128)(2,1)} %bitcast.10), calls=%async_computation.1 | async-start | bytes 4194304 | tf_op jit(solution)/shard_map/all_to_all | solution.py:184
  44.6 54.9 %copy-start.3 = (s32[1,512]{1,0:T(1,128)}, s32[1,512]{1,0:T(1,128)S(1)}, u32[]{:S(2)}) copy-start(s32[1,512]{1,0:T(1,128)S(1)} %get-tuple-element.19.place_ref) | copy-start | bytes 6148
  44.6 55.6 %copy-start = (bf16[1024,512]{1,0:T(8,128)(2,1)}, bf16[1024,512]{1,0:T(8,128)(2,1)S(1)}, u32[]{:S(2)}) copy-start(bf16[1024,512]{1,0:T(8,128)(2,1)S(1)} %get-tuple-element.26.refs_10_.refs_11_) | copy-start | bytes 3145732
  44.6 54.9 %collective-permute-start.6 = (bf16[1024,512]{1,0:T(8,128)(2,1)S(1)}, bf16[1024,512]{1,0:T(8,128)(2,1)}, u32[]{:S(2)}, u32[]{:S(2)}) collective-permute-start(bf16[1024,512]{1,0:T(8,128)(2,1)S(1)} %get-tuple-element.26.refs_10_.refs_11_), channel_id=1, source_target_pairs={{0,1},{2,3},{4,5},{6,7},{8,9},{10,11},{12,13},{14,15},{16,17},{18,... | collective-permute-start | bytes 3145736 | tf_op jit(solution)/shard_map/ppermute | solution.py:289
  48.7 15.4 %collective-permute-start.5 = (bf16[256,512]{1,0:T(8,128)(2,1)S(1)}, bf16[256,512]{1,0:T(8,128)(2,1)S(1)}, u32[]{:S(2)}, u32[]{:S(2)}) collective-permute-start(bf16[256,512]{1,0:T(8,128)(2,1)S(1)} %get-tuple-element.25), channel_id=1, source_target_pairs={{0,2},{1,3},{4,6},{5,7},{8,10},{9,11},{12,14},{13,15},{16,18},{17,... | collective-permute-start | bytes 786440 | tf_op jit(solution)/shard_map/ppermute | solution.py:288
  50.0 24.7 %collective-permute-start.2 = (bf16[256,512]{1,0:T(8,128)(2,1)S(1)}, bf16[256,512]{1,0:T(8,128)(2,1)S(1)}, u32[]{:S(2)}, u32[]{:S(2)}) collective-permute-start(bf16[256,512]{1,0:T(8,128)(2,1)S(1)} %get-tuple-element.22), channel_id=1, source_target_pairs={{0,2},{1,3},{4,6},{5,7},{8,10},{9,11},{12,14},{13,15},{16,18},{17,... | collective-permute-start | bytes 786440 | tf_op jit(solution)/shard_map/ppermute | solution.py:288
  51.3 29.8 %collective-permute-start.3 = (bf16[256,512]{1,0:T(8,128)(2,1)S(1)}, bf16[256,512]{1,0:T(8,128)(2,1)S(1)}, u32[]{:S(2)}, u32[]{:S(2)}) collective-permute-start(bf16[256,512]{1,0:T(8,128)(2,1)S(1)} %get-tuple-element.23), channel_id=1, source_target_pairs={{0,2},{1,3},{4,6},{5,7},{8,10},{9,11},{12,14},{13,15},{16,18},{17,... | collective-permute-start | bytes 786440 | tf_op jit(solution)/shard_map/ppermute | solution.py:288
  52.6 36.2 %collective-permute-start.4 = (bf16[256,512]{1,0:T(8,128)(2,1)S(1)}, bf16[256,512]{1,0:T(8,128)(2,1)S(1)}, u32[]{:S(2)}, u32[]{:S(2)}) collective-permute-start(bf16[256,512]{1,0:T(8,128)(2,1)S(1)} %get-tuple-element.24), channel_id=1, source_target_pairs={{0,2},{1,3},{4,6},{5,7},{8,10},{9,11},{12,14},{13,15},{16,18},{17,... | collective-permute-start | bytes 786440 | tf_op jit(solution)/shard_map/ppermute | solution.py:288
  64.1 36.1 %copy-start.4 = (bf16[256,512]{1,0:T(8,128)(2,1)}, bf16[256,512]{1,0:T(8,128)(2,1)S(1)}, u32[]{:S(2)}) copy-start(bf16[256,512]{1,0:T(8,128)(2,1)S(1)} %collective-permute-done.5.refs_3_) | copy-start | bytes 786436
  64.1 25.9 %collective-permute-start.10 = (bf16[256,512]{1,0:T(8,128)(2,1)S(1)}, bf16[256,512]{1,0:T(8,128)(2,1)S(1)}, u32[]{:S(2)}, u32[]{:S(2)}) collective-permute-start(bf16[256,512]{1,0:T(8,128)(2,1)S(1)} %collective-permute-done.5.refs_3_), channel_id=1, source_target_pairs={{3,2},{7,6},{11,10},{15,14},{19,18},{23,22},{27,26},{31,30}} | collective-permute-start | bytes 786440 | tf_op jit(solution)/shard_map/ppermute | solution.py:290
  74.7 25.5 %copy-start.5 = (bf16[256,512]{1,0:T(8,128)(2,1)}, bf16[256,512]{1,0:T(8,128)(2,1)S(1)}, u32[]{:S(2)}) copy-start(bf16[256,512]{1,0:T(8,128)(2,1)S(1)} %collective-permute-done.2.refs_0_) | copy-start | bytes 786436
  74.7 15.4 %collective-permute-start.7 = (bf16[256,512]{1,0:T(8,128)(2,1)S(1)}, bf16[256,512]{1,0:T(8,128)(2,1)S(1)}, u32[]{:S(2)}, u32[]{:S(2)}) collective-permute-start(bf16[256,512]{1,0:T(8,128)(2,1)S(1)} %collective-permute-done.2.refs_0_), channel_id=1, source_target_pairs={{3,2},{7,6},{11,10},{15,14},{19,18},{23,22},{27,26},{31,30}} | collective-permute-start | bytes 786440 | tf_op jit(solution)/shard_map/ppermute | solution.py:290
  81.1 19.1 %copy-start.6 = (bf16[256,512]{1,0:T(8,128)(2,1)}, bf16[256,512]{1,0:T(8,128)(2,1)S(1)}, u32[]{:S(2)}) copy-start(bf16[256,512]{1,0:T(8,128)(2,1)S(1)} %collective-permute-done.3.refs_1_) | copy-start | bytes 786436
  81.1 12.8 %collective-permute-start.8 = (bf16[256,512]{1,0:T(8,128)(2,1)S(1)}, bf16[256,512]{1,0:T(8,128)(2,1)S(1)}, u32[]{:S(2)}, u32[]{:S(2)}) collective-permute-start(bf16[256,512]{1,0:T(8,128)(2,1)S(1)} %collective-permute-done.3.refs_1_), channel_id=1, source_target_pairs={{3,2},{7,6},{11,10},{15,14},{19,18},{23,22},{27,26},{31,30}} | collective-permute-start | bytes 786440 | tf_op jit(solution)/shard_map/ppermute | solution.py:290
  88.7 5.1 %copy-start.7 = (bf16[256,512]{1,0:T(8,128)(2,1)}, bf16[256,512]{1,0:T(8,128)(2,1)S(1)}, u32[]{:S(2)}) copy-start(bf16[256,512]{1,0:T(8,128)(2,1)S(1)} %collective-permute-done.4.refs_2_) | copy-start | bytes 786436
  88.7 10.8 %collective-permute-start.9 = (bf16[256,512]{1,0:T(8,128)(2,1)S(1)}, bf16[256,512]{1,0:T(8,128)(2,1)S(1)}, u32[]{:S(2)}, u32[]{:S(2)}) collective-permute-start(bf16[256,512]{1,0:T(8,128)(2,1)S(1)} %collective-permute-done.4.refs_2_), channel_id=1, source_target_pairs={{3,2},{7,6},{11,10},{15,14},{19,18},{23,22},{27,26},{31,30}} | collective-permute-start | bytes 786440 | tf_op jit(solution)/shard_map/ppermute | solution.py:290
  90.0 9.5 %copy-start.8 = (bf16[256,512]{1,0:T(8,128)(2,1)}, bf16[256,512]{1,0:T(8,128)(2,1)S(1)}, u32[]{:S(2)}) copy-start(bf16[256,512]{1,0:T(8,128)(2,1)S(1)} %collective-permute-done.10.refs_9_) | copy-start | bytes 786436
  90.1 9.4 %copy-start.9 = (bf16[256,512]{1,0:T(8,128)(2,1)}, bf16[256,512]{1,0:T(8,128)(2,1)S(1)}, u32[]{:S(2)}) copy-start(bf16[256,512]{1,0:T(8,128)(2,1)S(1)} %collective-permute-done.7.refs_6_) | copy-start | bytes 786436
  93.9 5.6 %copy-start.10 = (bf16[256,512]{1,0:T(8,128)(2,1)}, bf16[256,512]{1,0:T(8,128)(2,1)S(1)}, u32[]{:S(2)}) copy-start(bf16[256,512]{1,0:T(8,128)(2,1)S(1)} %collective-permute-done.8.refs_7_) | copy-start | bytes 786436
  99.5 0.7 copy-start.11
where the time goes:
time: 119 us
  waiting for transfers between devices  57.3 us (48%)
  starting transfers between devices  28.9 us (24%)
  Pallas kernels  26.7 us (22%)
  other arithmetic  2.44 us (2%)
  between operations  2.31 us (2%)
  local copies, waits for them, and re-layouts  1.24 us (1%)
    ppermute x4, waiting for transfers between devices, per_device(): far = [lax.ppermute(x, 'ctx', [(0, 2), (1, 3)]) for x in pieces]  31 us
    pallas_call x1, Pallas kernels, attend(): pl.pallas_call(functools.partial(attend_kernel, sources), out_shape=jax.S...  18.5 us
    all_to_all x2, waiting for transfers between devices, all_to_all(): lax.all_to_all(x, ('dp', 'ctx'), split_axis=0, concat_axis=0, tiled=True)  13.8 us
    all_to_all x2, starting transfers between devices, all_to_all(): lax.all_to_all(x, ('dp', 'ctx'), split_axis=0, concat_axis=0, tiled=True)  10.2 us
    ppermute x4, waiting for transfers between devices, per_device(): hop = [lax.ppermute(x, 'ctx', [(3, 2)]) for x in far]  9.42 us
    ppermute x4, starting transfers between devices, per_device(): far = [lax.ppermute(x, 'ctx', [(0, 2), (1, 3)]) for x in pieces]  5.16 us
    ppermute x4, starting transfers between devices, per_device(): hop = [lax.ppermute(x, 'ctx', [(3, 2)]) for x in far]  5.12 us
    ppermute x2, starting transfers between devices, from_before(): lax.ppermute(x, 'ctx', [(i, i + distance) for i in range(ctx_size - dista...  4.38 us
  transfers between devices with their start and end apart: 13, of which 9 were waited for; matrix products, arithmetic and copies ran while one was open for 2% of the time, Pallas kernels for 4%

commit v1 on v0

--- a/solution.py
+++ b/solution.py
@@ -16,6 +16,7 @@
 GROUP_COLS = GROUP * HD
 META = 128
 STEP = 256
+VMEM_ATTEND = 62
 NEG = -1e30
 MIB = 1 << 20
 
@@ -85,38 +86,36 @@
 
 def attend_kernel(sources, early_ref, place_ref, start_ref, q_ref, *refs):
     kv_refs = refs[:-7]
-    out_ref, matrix_ref, bias_ref, q_buf, key_buf, value_buf, score_buf = refs[-7:]
+    out_ref, bias_ref, q_buf, key_buf, value_buf, even_buf, odd_buf = refs[-7:]
     rows = q_ref.shape[0]
     width = key_buf.shape[0]
+    tiles = rows // STEP
     begin = width - rows
     scale = math.log2(math.e) / math.sqrt(HD)
     first, early_steps, all_early = early_ref[0], early_ref[1], early_ref[2]
 
-    @pl.when(pl.program_id(0) == 0)
-    def _():
-        matrix_ref[...] = (iota((rows, rows), 0) == place_ref[...]).astype(BF16)
-        key, query = iota((rows, rows), 0), iota((rows, rows), 1)
-        allowed = (key + begin >= start_ref[...]) & (key <= query)
-        bias_ref[...] = jnp.where(allowed, 0.0, NEG)
-        value_buf[HD:, :] = jnp.ones((value_buf.shape[0] - HD, width), BF16)
-
-    q_buf[...] = dot(matrix_ref[...], q_ref[...]).astype(BF16)
-    group, at = pl.program_id(0), 0
+    matrix = (iota((rows, rows), 0) == place_ref[...]).astype(BF16)
+    for g in range(KV_HEADS):
+        columns = slice(g * GROUP_COLS, (g + 1) * GROUP_COLS)
+        q_buf[:, columns] = dot(matrix, q_ref[:, columns]).astype(BF16)
+    key, query = iota((rows, rows), 0), iota((rows, rows), 1)
+    allowed = (key + begin >= start_ref[...]) & (key <= query)
+    bias_ref[...] = jnp.where(allowed, 0.0, NEG)
+
+    at = 0
     for b, block in enumerate(sources):
-        keys, values = [], []
+        here = slice(b * rows, (b + 1) * rows)
+        parts = []
         for count in block:
-            refs_here = kv_refs[at : at + count]
+            parts.append([ref[...] for ref in kv_refs[at : at + count]])
+            parts[-1] = jnp.concatenate(parts[-1], axis=0) if count > 1 else parts[-1][0]
             at += count
-            if count == 2:
-                key, value = (ref[...] for ref in refs_here)
-            else:
-                key = jnp.concatenate([ref[...] for ref in refs_here[:2]], axis=0)
-                value = jnp.where(group < KV_HEADS // 2, refs_here[2][...], refs_here[3][...])
-            keys.append(key)
-            values.append(value)
-        here = slice(b * rows, (b + 1) * rows)
-        key_buf[here, :] = sum(keys[1:], keys[0])
-        value_buf[:HD, here] = sum(values[1:], values[0])
+        kv = sum(parts[1:], parts[0])
+        key_buf[here, :] = kv[:rows]
+        for g in range(KV_HEADS):
+            value_buf[g, :HD, here] = kv[rows + g * HD : rows + (g + 1) * HD]
+    for g in range(KV_HEADS):
+        value_buf[g, HD:, :] = jnp.ones((value_buf.shape[1] - HD, width), BF16)
 
     def run(counts):
         def steps_of(tile):
@@ -125,55 +124,62 @@
         def queries_of(tile):
             return slice(tile * STEP, (tile + 1) * STEP)
 
-        def score(slot, tile, h, i, at, tops):
+        def columns(index):
+            return pl.ds(pl.multiple_of(index * HD, HD), HD)
+
+        def score(buf, head, tile, i, at, tops):
             part = dot_nt(
-                key_buf[at : at + STEP, :], q_buf[queries_of(tile), h * HD : (h + 1) * HD]
+                key_buf[at : at + STEP, columns(head // GROUP)],
+                q_buf[queries_of(tile), columns(head)],
             )
             own = at >= begin
             if own:
                 part = part + bias_ref[at - begin : at - begin + STEP, queries_of(tile)]
             elif i == 0:
                 part = jnp.where(iota((STEP, 1), 0) + at >= first, part, NEG)
-            score_buf[slot, i * STEP : (i + 1) * STEP, :] = part
+            buf[tile, i * STEP : (i + 1) * STEP, :] = part
             peak = jnp.max(part.reshape(STEP // 8, 8, STEP), axis=0)
             tops[own] = jnp.maximum(tops[own], peak) if own in tops else peak
 
         def largest_of(tile, tops):
             own = jnp.max(tops[True], axis=0, keepdims=True)
             if False not in tops:
-                return {True: own}
+                return own, own
             shared = jnp.where(start_ref[:, queries_of(tile)] == first, 0.0, -NEG)
             early = jnp.max(tops[False], axis=0, keepdims=True)
             both = jnp.maximum(own, early - shared)
-            return {True: both, False: both + shared}
-
-        def weigh(slot, i, at, largest, summed):
-            part = score_buf[slot, i * STEP : (i + 1) * STEP, :]
-            probs = jnp.exp2((part - largest[at >= begin]) * scale).astype(BF16)
-            added = dot(value_buf[:, at : at + STEP], probs)
+            return both, both + shared
+
+        def weigh(buf, head, tile, i, at, largest, summed):
+            part = buf[tile, i * STEP : (i + 1) * STEP, :]
+            probs = jnp.exp2((part - largest[int(at < begin)]) * scale).astype(BF16)
+            added = dot(value_buf[head // GROUP, :, at : at + STEP], probs)
             return added if summed is None else summed + added
 
-        def finish(tile, h, summed):
+        def finish(head, tile, summed):
             result = (summed[:HD] * (1.0 / summed[HD : HD + 1])).astype(BF16)
-            out_ref[queries_of(tile), h * HD : (h + 1) * HD] = result.T
-
-        chains = [(tile, h) for tile in range(rows // STEP) for h in range(GROUP)]
-        largest = {}
-        for c in range(len(chains) + 1):
-            tops, summed = {}, None
-            now = steps_of(chains[c][0]) if c < len(chains) else []
-            past = steps_of(chains[c - 1][0]) if c else []
-            for i in range(max(len(now), len(past))):
-                if i < len(now):
-                    score(c % 2, *chains[c], i, now[i], tops)
-                if i < len(past):
-                    summed = weigh((c - 1) % 2, i, past[i], largest[c - 1], summed)
-            if now:
-                largest[c] = largest_of(chains[c][0], tops)
-            if past:
-                finish(*chains[c - 1], summed)
-
-    tiles = rows // STEP
+            out_ref[queries_of(tile), columns(head)] = result.T
+
+        def both(next_buf, next_head, buf, head, largest):
+            coming = []
+            for tile in range(tiles):
+                tops, summed = {}, None
+                for i, at in enumerate(steps_of(tile)):
+                    if head is not None:
+                        summed = weigh(buf, head, tile, i, at, largest[tile], summed)
+                    score(next_buf, next_head, tile, i, at, tops)
+                if head is not None:
+                    finish(head, tile, summed)
+                coming.append(largest_of(tile, tops))
+            return tuple(coming)
+
+        def two_heads(pair, largest):
+            head = 2 * pair
+            largest = both(odd_buf, head + 1, even_buf, head, largest)
+            return both(even_buf, jnp.minimum(head + 2, HEADS - 1), odd_buf, head + 1, largest)
+
+        lax.fori_loop(0, HEADS // 2, two_heads, both(even_buf, 0, None, None, None))
+
     for early in range(begin // STEP + 1):
         for whole in (False, True) if early else (True,):
             counts = [early if whole or t == 0 else 0 for t in range(tiles)]
@@ -186,40 +192,22 @@
 
 def attend(early, place, start, q_got, kv):
     rows = q_got.shape[0]
-    blocks = len(kv)
-    width = blocks * rows
-    keys_of = pl.BlockSpec((rows, HD), lambda g, *_: (0, g))
-    values_of = pl.BlockSpec((HD, rows), lambda g, *_: (rows // HD + g, 0))
-    keys_of_half = pl.BlockSpec((rows // 2, HD), lambda g, *_: (0, g))
-    values_of_half = pl.BlockSpec((HD, rows), lambda g, *_: (g % (KV_HEADS // 2), 0))
-    arrays, specs = [], []
-    for block in kv:
-        for source in block:
-            one = len(source) == 1
-            arrays += list(source) * 2 if one else list(source)
-            specs += [keys_of, values_of] if one else [keys_of_half] * 2 + [values_of_half] * 2
-    sources = [[2 if len(source) == 1 else 4 for source in block] for block in kv]
-    whole = lambda shape: pl.BlockSpec(shape, lambda g, *_: (0, 0))
+    width = len(kv) * rows
+    arrays = [x for block in kv for source in block for x in source]
     return pl.pallas_call(
-        functools.partial(attend_kernel, sources),
+        functools.partial(attend_kernel, [[len(source) for source in block] for block in kv]),
         out_shape=jax.ShapeDtypeStruct(q_got.shape, BF16),
-        grid_spec=pltpu.PrefetchScalarGridSpec(
-            num_scalar_prefetch=1,
-            grid=(KV_HEADS,),
-            in_specs=[whole((1, rows)), whole((1, rows))]
-            + [pl.BlockSpec((rows, GROUP_COLS), lambda g, *_: (0, g))]
-            + specs,
-            out_specs=pl.BlockSpec((rows, GROUP_COLS), lambda g, *_: (0, g)),
-            scratch_shapes=[
-                pltpu.VMEM((rows, rows), BF16),
-                pltpu.VMEM((rows, rows), F32),
-                pltpu.VMEM((rows, GROUP_COLS), BF16),
-                pltpu.VMEM((width, HD), BF16),
-                pltpu.VMEM((HD + 16, width), BF16),
-                pltpu.VMEM((2, width, STEP), F32),
-            ],
-        ),
-        compiler_params=pltpu.CompilerParams(vmem_limit_bytes=62 * MIB),
+        in_specs=[pl.BlockSpec(memory_space=pltpu.SMEM)]
+        + [pl.BlockSpec(memory_space=pltpu.VMEM)] * (3 + len(arrays)),
+        scratch_shapes=[
+            pltpu.VMEM((rows, rows), F32),
+            pltpu.VMEM(q_got.shape, BF16),
+            pltpu.VMEM((width, KV_HEADS * HD), BF16),
+            pltpu.VMEM((KV_HEADS, HD + 16, width), BF16),
+            pltpu.VMEM((rows // STEP, width, STEP), F32),
+            pltpu.VMEM((rows // STEP, width, STEP), F32),
+        ],
+        compiler_params=pltpu.CompilerParams(vmem_limit_bytes=VMEM_ATTEND * MIB),
         name="attend",
     )(early, place, start, q_got, *arrays)
 
@@ -247,8 +235,9 @@
     def from_before(x, distance):
         return lax.ppermute(x, "ctx", [(i, i + distance) for i in range(ctx_size - distance)])
 
-    kv_out, docs = lax.optimization_barrier((kv_out, doc_ids.reshape(rows) + 1))
+    kv_out, docs = lax.optimization_barrier((kv_out, doc_ids))
     kv_got = all_to_all(kv_out)
+    docs = docs.reshape(rows) + 1
 
     doc_line = jnp.concatenate([from_before(docs, d) for d in range(before, 0, -1)] + [docs])
     start = jnp.sum((doc_line[None, :] < docs[:, None]).astype(jnp.int32), axis=1)

time: 119 us -> 117 us (0.983)
  the two profiles are of different devices: /device:TPU:5 before, /device:TPU:20 now
where the time goes in v1:
time: 117 us; the launch traced here: 115 us
  waiting for transfers between devices  55.2 us (47%)
  starting transfers between devices  31 us (26%)
  Pallas kernels  23.6 us (20%)
  between operations  2.18 us (2%)
  other arithmetic  1.74 us (1%)
  local copies, waits for them, and re-layouts  1.29 us (1%)
    ppermute x4, waiting for transfers between devices, per_device(): far = [lax.ppermute(x, 'ctx', [(0, 2), (1, 3)]) for x in pieces]  32.5 us
    pallas_call x1, Pallas kernels, attend(): pl.pallas_call(functools.partial(attend_kernel, [[len(source) for source...  15.4 us
    all_to_all x2, starting transfers between devices, all_to_all(): lax.all_to_all(x, ('dp', 'ctx'), split_axis=0, concat_axis=0, tiled=True)  11.6 us
    all_to_all x2, waiting for transfers between devices, all_to_all(): lax.all_to_all(x, ('dp', 'ctx'), split_axis=0, concat_axis=0, tiled=True)  10.8 us
    ppermute x4, waiting for transfers between devices, per_device(): hop = [lax.ppermute(x, 'ctx', [(3, 2)]) for x in far]  8.22 us
    ppermute x4, starting transfers between devices, per_device(): far = [lax.ppermute(x, 'ctx', [(0, 2), (1, 3)]) for x in pieces]  5.16 us
    ppermute x4, starting transfers between devices, per_device(): hop = [lax.ppermute(x, 'ctx', [(3, 2)]) for x in far]  5.12 us
    ppermute x2, starting transfers between devices, from_before(): lax.ppermute(x, 'ctx', [(i, i + distance) for i in range(ctx_size - dista...  4.68 us
  transfers between devices with their start and end apart: 13, of which 9 were waited for; matrix products, arithmetic and copies ran while one was open for 2% of the time, Pallas kernels for 4%

profile of v1, /device:TPU:20, one launch (start us, length us, event | category | flops | bytes accessed | tf_op | source)
XLA Modules:
  0.0 115.0 jit_solution(1194655644897407304)
XLA Ops:
  0.0 0.0 copy-start.13
  0.0 0.0 copy-start
  0.0 0.0 copy-start.2
  0.0 3.8 %pack_kv.1 = bf16[512,1152]{1,0:T(8,128)(2,1)} custom-call(s32[1,512]{1,0:T(1,128)} %bitcast.13, bf16[512,1024]{1,0:T(8,128)(2,1)} %kv_hbm.1), custom_call_target="tpu_custom_call" | custom-call | tf_op jit(solution)/shard_map/pack_kv/pallas_call | solution.py:226
  3.8 5.9 %all-to-all-start = ((bf16[32,16,1152]{2,1,0:T(8,128)(2,1)}), bf16[32,16,1152]{2,1,0:T(8,128)(2,1)S(1)}, u32[]{:S(2)}, u32[]{:S(2)}) async-start(bf16[32,16,1152]{2,1,0:T(8,128)(2,1)} %bitcast.15), calls=%async_computation | async-start | bytes 2359296 | tf_op jit(solution)/shard_map/all_to_all | solution.py:190
  9.7 0.0 copy-done.13
  9.8 1.3 %collective-permute-start = (s32[512]{0:T(512)S(1)}, s32[512]{0:T(512)S(1)}, u32[]{:S(2)}, u32[]{:S(2)}) collective-permute-start(s32[512]{0:T(512)S(1)} %bitcast.16), channel_id=1, source_target_pairs={{0,2},{1,3},{4,6},{5,7},{8,10},{9,11},{12,14},{13,15},{16,18},{17,... | collective-permute-start | bytes 6152 | tf_op jit(solution)/shard_map/ppermute | solution.py:236
  11.1 3.4 %collective-permute-start.1 = (s32[512]{0:T(512)S(1)}, s32[512]{0:T(512)S(1)}, u32[]{:S(2)}, u32[]{:S(2)}) collective-permute-start(s32[512]{0:T(512)S(1)} %bitcast.17), channel_id=1, source_target_pairs={{0,1},{1,2},{2,3},{4,5},{5,6},{6,7},{8,9},{9,10},{10,11},{12,13},{... | collective-permute-start | bytes 6152 | tf_op jit(solution)/shard_map/ppermute | solution.py:236
  14.5 1.3 %collective-permute-done = s32[512]{0:T(512)S(1)} collective-permute-done((s32[512]{0:T(512)S(1)}, s32[512]{0:T(512)S(1)}, u32[]{:S(2)}, u32[]{:S(2)}) %collective-permute-start) | collective-permute-done | bytes 2080 | tf_op jit(solution)/shard_map/ppermute | solution.py:236
  15.8 2.4 %collective-permute-done.1 = s32[512]{0:T(512)S(1)} collective-permute-done((s32[512]{0:T(512)S(1)}, s32[512]{0:T(512)S(1)}, u32[]{:S(2)}, u32[]{:S(2)}) %collective-permute-start.1) | collective-permute-done | bytes 2080 | tf_op jit(solution)/shard_map/ppermute | solution.py:236
  18.2 0.5 convert_reduce_fusion
  18.7 0.0 copy-start.12
  18.7 0.6 fusion
  21.2 1.2 %pad_add_fusion.1.early_ref = s32[3]{0:T(128)} fusion(s32[1]{0:T(128)} %bitcast.6, s32[1]{0:T(128)} %bitcast.4, s32[1]{0:T(128)} %get-tuple-element.27), kind=kLoop, calls=%fused_computation.3 | loop fusion | flops 6 | bytes 24 | tf_op jit(solution)/shard_map/stack | solution.py:248
  22.4 0.0 copy-done
  22.4 0.0 copy-done.2
  22.4 3.5 %pack_q.1 = bf16[512,2048]{1,0:T(8,128)(2,1)} custom-call(s32[1,512]{1,0:T(1,128)S(1)} %bitcast.14, bf16[512,2048]{1,0:T(8,128)(2,1)S(1)} %copy-done), custom_call_target="tpu_custom_call" | custom-call | tf_op jit(solution)/shard_map/pack_q/pallas_call | solution.py:251
  25.9 0.0 copy-done.12
  25.9 10.8 %all-to-all-done = bf16[32,16,1152]{2,1,0:T(8,128)(2,1)S(1)} async-done(((bf16[32,16,1152]{2,1,0:T(8,128)(2,1)}), bf16[32,16,1152]{2,1,0:T(8,128)(2,1)S(1)}, u32[]{:S(2)}, u32[]{:S(2)}) %all-to-all-start) | async-done | bytes 1179680 | tf_op jit(solution)/shard_map/all_to_all | solution.py:190
  36.7 5.7 %all-to-all-start.1 = ((bf16[32,16,2048]{2,1,0:T(8,128)(2,1)}), bf16[32,16,2048]{2,1,0:T(8,128)(2,1)}, u32[]{:S(2)}, u32[]{:S(2)}) async-start(bf16[32,16,2048]{2,1,0:T(8,128)(2,1)} %bitcast.10), calls=%async_computation.1 | async-start | bytes 4194304 | tf_op jit(solution)/shard_map/all_to_all | solution.py:190
  42.5 0.9 sort_kv.1
  43.4 0.0 copy-start.3
  43.4 0.0 copy-start.1
  43.4 4.4 %collective-permute-start.6 = (bf16[1024,512]{1,0:T(8,128)(2,1)S(1)}, bf16[1024,512]{1,0:T(8,128)(2,1)}, u32[]{:S(2)}, u32[]{:S(2)}) collective-permute-start(bf16[1024,512]{1,0:T(8,128)(2,1)S(1)} %get-tuple-element.26.refs_9_), channel_id=1, source_target_pairs={{0,1},{2,3},{4,5},{6,7},{8,9},{10,11},{12,13},{14,15},{16,17},{18,... | collective-permute-start | bytes 3145736 | tf_op jit(solution)/shard_map/ppermute | solution.py:278
  47.8 1.3 %collective-permute-start.5 = (bf16[256,512]{1,0:T(8,128)(2,1)S(1)}, bf16[256,512]{1,0:T(8,128)(2,1)S(1)}, u32[]{:S(2)}, u32[]{:S(2)}) collective-permute-start(bf16[256,512]{1,0:T(8,128)(2,1)S(1)} %get-tuple-element.25), channel_id=1, source_target_pairs={{0,2},{1,3},{4,6},{5,7},{8,10},{9,11},{12,14},{13,15},{16,18},{17,... | collective-permute-start | bytes 786440 | tf_op jit(solution)/shard_map/ppermute | solution.py:277
  49.1 1.3 %collective-permute-start.2 = (bf16[256,512]{1,0:T(8,128)(2,1)S(1)}, bf16[256,512]{1,0:T(8,128)(2,1)S(1)}, u32[]{:S(2)}, u32[]{:S(2)}) collective-permute-start(bf16[256,512]{1,0:T(8,128)(2,1)S(1)} %get-tuple-element.22), channel_id=1, source_target_pairs={{0,2},{1,3},{4,6},{5,7},{8,10},{9,11},{12,14},{13,15},{16,18},{17,... | collective-permute-start | bytes 786440 | tf_op jit(solution)/shard_map/ppermute | solution.py:277
  50.4 1.3 %collective-permute-start.3 = (bf16[256,512]{1,0:T(8,128)(2,1)S(1)}, bf16[256,512]{1,0:T(8,128)(2,1)S(1)}, u32[]{:S(2)}, u32[]{:S(2)}) collective-permute-start(bf16[256,512]{1,0:T(8,128)(2,1)S(1)} %get-tuple-element.23), channel_id=1, source_target_pairs={{0,2},{1,3},{4,6},{5,7},{8,10},{9,11},{12,14},{13,15},{16,18},{17,... | collective-permute-start | bytes 786440 | tf_op jit(solution)/shard_map/ppermute | solution.py:277
  51.7 1.3 %collective-permute-start.4 = (bf16[256,512]{1,0:T(8,128)(2,1)S(1)}, bf16[256,512]{1,0:T(8,128)(2,1)S(1)}, u32[]{:S(2)}, u32[]{:S(2)}) collective-permute-start(bf16[256,512]{1,0:T(8,128)(2,1)S(1)} %get-tuple-element.24), channel_id=1, source_target_pairs={{0,2},{1,3},{4,6},{5,7},{8,10},{9,11},{12,14},{13,15},{16,18},{17,... | collective-permute-start | bytes 786440 | tf_op jit(solution)/shard_map/ppermute | solution.py:277
  53.0 12.7 %collective-permute-done.5.refs_3_ = bf16[256,512]{1,0:T(8,128)(2,1)S(1)} collective-permute-done((bf16[256,512]{1,0:T(8,128)(2,1)S(1)}, bf16[256,512]{1,0:T(8,128)(2,1)S(1)}, u32[]{:S(2)}, u32[]{:S(2)}) %collective-permute-start.5) | collective-permute-done | bytes 262176 | tf_op jit(solution)/shard_map/ppermute | solution.py:277
  65.7 0.0 copy-start.4
  65.7 1.3 %collective-permute-start.10 = (bf16[256,512]{1,0:T(8,128)(2,1)S(1)}, bf16[256,512]{1,0:T(8,128)(2,1)S(1)}, u32[]{:S(2)}, u32[]{:S(2)}) collective-permute-start(bf16[256,512]{1,0:T(8,128)(2,1)S(1)} %collective-permute-done.5.refs_3_), channel_id=1, source_target_pairs={{3,2},{7,6},{11,10},{15,14},{19,18},{23,22},{27,26},{31,30}} | collective-permute-start | bytes 786440 | tf_op jit(solution)/shard_map/ppermute | solution.py:279
  67.0 7.6 %collective-permute-done.2.refs_0_ = bf16[256,512]{1,0:T(8,128)(2,1)S(1)} collective-permute-done((bf16[256,512]{1,0:T(8,128)(2,1)S(1)}, bf16[256,512]{1,0:T(8,128)(2,1)S(1)}, u32[]{:S(2)}, u32[]{:S(2)}) %collective-permute-start.2) | collective-permute-done | bytes 262176 | tf_op jit(solution)/shard_map/ppermute | solution.py:277
  74.6 0.0 copy-start.5
  74.6 1.3 %collective-permute-start.7 = (bf16[256,512]{1,0:T(8,128)(2,1)S(1)}, bf16[256,512]{1,0:T(8,128)(2,1)S(1)}, u32[]{:S(2)}, u32[]{:S(2)}) collective-permute-start(bf16[256,512]{1,0:T(8,128)(2,1)S(1)} %collective-permute-done.2.refs_0_), channel_id=1, source_target_pairs={{3,2},{7,6},{11,10},{15,14},{19,18},{23,22},{27,26},{31,30}} | collective-permute-start | bytes 786440 | tf_op jit(solution)/shard_map/ppermute | solution.py:279
  75.9 8.1 %collective-permute-done.3.refs_1_ = bf16[256,512]{1,0:T(8,128)(2,1)S(1)} collective-permute-done((bf16[256,512]{1,0:T(8,128)(2,1)S(1)}, bf16[256,512]{1,0:T(8,128)(2,1)S(1)}, u32[]{:S(2)}, u32[]{:S(2)}) %collective-permute-start.3) | collective-permute-done | bytes 262176 | tf_op jit(solution)/shard_map/ppermute | solution.py:277
  83.9 0.0 copy-start.6
  83.9 1.3 %collective-permute-start.8 = (bf16[256,512]{1,0:T(8,128)(2,1)S(1)}, bf16[256,512]{1,0:T(8,128)(2,1)S(1)}, u32[]{:S(2)}, u32[]{:S(2)}) collective-permute-start(bf16[256,512]{1,0:T(8,128)(2,1)S(1)} %collective-permute-done.3.refs_1_), channel_id=1, source_target_pairs={{3,2},{7,6},{11,10},{15,14},{19,18},{23,22},{27,26},{31,30}} | collective-permute-start | bytes 786440 | tf_op jit(solution)/shard_map/ppermute | solution.py:279
  85.2 4.1 %collective-permute-done.4.refs_2_ = bf16[256,512]{1,0:T(8,128)(2,1)S(1)} collective-permute-done((bf16[256,512]{1,0:T(8,128)(2,1)S(1)}, bf16[256,512]{1,0:T(8,128)(2,1)S(1)}, u32[]{:S(2)}, u32[]{:S(2)}) %collective-permute-start.4) | collective-permute-done | bytes 262176 | tf_op jit(solution)/shard_map/ppermute | solution.py:277
  89.4 0.0 copy-start.7
  89.4 1.3 %collective-permute-start.9 = (bf16[256,512]{1,0:T(8,128)(2,1)S(1)}, bf16[256,512]{1,0:T(8,128)(2,1)S(1)}, u32[]{:S(2)}, u32[]{:S(2)}) collective-permute-start(bf16[256,512]{1,0:T(8,128)(2,1)S(1)} %collective-permute-done.4.refs_2_), channel_id=1, source_target_pairs={{3,2},{7,6},{11,10},{15,14},{19,18},{23,22},{27,26},{31,30}} | collective-permute-start | bytes 786440 | tf_op jit(solution)/shard_map/ppermute | solution.py:279
  90.6 0.0 collective-permute-done.10.refs_8_
  90.7 0.0 copy-start.8
  90.7 0.0 collective-permute-done.7.refs_5_
  90.7 0.0 copy-start.9
  90.7 2.7 %collective-permute-done.8.refs_6_ = bf16[256,512]{1,0:T(8,128)(2,1)S(1)} collective-permute-done((bf16[256,512]{1,0:T(8,128)(2,1)S(1)}, bf16[256,512]{1,0:T(8,128)(2,1)S(1)}, u32[]{:S(2)}, u32[]{:S(2)}) %collective-permute-start.8) | collective-permute-done | bytes 262176 | tf_op jit(solution)/shard_map/ppermute | solution.py:279
  93.3 0.0 copy-done.7
  93.3 0.0 copy-start.10
  93.4 5.6 %collective-permute-done.9.refs_7_ = bf16[256,512]{1,0:T(8,128)(2,1)S(1)} collective-permute-done((bf16[256,512]{1,0:T(8,128)(2,1)S(1)}, bf16[256,512]{1,0:T(8,128)(2,1)S(1)}, u32[]{:S(2)}, u32[]{:S(2)}) %collective-permute-start.9) | collective-permute-done | bytes 262176 | tf_op jit(solution)/shard_map/ppermute | solution.py:279
  98.9 0.0 copy-done.8
  98.9 0.0 copy-done.9
  98.9 0.0 copy-done.10
  98.9 0.0 copy-start.11
  98.9 0.0 collective-permute-done.6.refs_4_
  98.9 0.0 copy-done.3
  98.9 0.0 all-to-all-done.1
  99.0 0.7 copy-done.11
  99.6 0.0 copy-done.1
  99.6 0.0 copy-done.4
  99.6 0.0 copy-done.5
  99.6 0.0 copy-done.6
  99.6 15.4 %attend.1 = bf16[512,2048]{1,0:T(8,128)(2,1)} custom-call(s32[3]{0:T(128)} %pad_add_fusion.1.early_ref, s32[1,512]{1,0:T(1,128)} %copy-done.3, s32[1,512]{1,0:T(1,128)} %bitcast.20, bf16[512,2048]{1,0:T(8,128)(2,1)} %bitcast.11.q_ref, bf16[256,512]{1,0:T(8,128)(2,1)} %copy-done.5, bf16[256,512]{1,0:T(8,128)(2,1)} %copy-done.6, bf16[256,512]{1,0:T(8,128)(2,1)} %copy-done.7, ...), custom_call_target="tpu_custom_call" | custom-call | tf_op jit(solution)/shard_map/attend/pallas_call | solution.py:197
  (2 shorter events, 0.0 us)
Async XLA Ops:
  0.0 9.7 %copy-start.13 = (s32[1,512]{1,0:T(1,128)S(1)}, s32[1,512]{1,0:T(1,128)}, u32[]{:S(2)}) copy-start(s32[1,512]{1,0:T(1,128)} %param.7) | copy-start | bytes 6148
  0.0 22.4 %copy-start = (bf16[512,2048]{1,0:T(8,128)(2,1)S(1)}, bf16[512,2048]{1,0:T(8,128)(2,1)}, u32[]{:S(2)}) copy-start(bf16[512,2048]{1,0:T(8,128)(2,1)} %q_ref) | copy-start | bytes 6291460
  0.0 22.4 %copy-start.2 = (s32[512]{0:T(512)S(1)}, s32[512]{0:T(512)}, u32[]{:S(2)}) copy-start(s32[512]{0:T(512)} %param.6) | copy-start | bytes 6148
  3.8 32.9 %all-to-all-start = ((bf16[32,16,1152]{2,1,0:T(8,128)(2,1)}), bf16[32,16,1152]{2,1,0:T(8,128)(2,1)S(1)}, u32[]{:S(2)}, u32[]{:S(2)}) async-start(bf16[32,16,1152]{2,1,0:T(8,128)(2,1)} %bitcast.15), calls=%async_computation | async-start | bytes 2359296 | tf_op jit(solution)/shard_map/all_to_all | solution.py:190
  9.8 6.0 %collective-permute-start = (s32[512]{0:T(512)S(1)}, s32[512]{0:T(512)S(1)}, u32[]{:S(2)}, u32[]{:S(2)}) collective-permute-start(s32[512]{0:T(512)S(1)} %bitcast.16), channel_id=1, source_target_pairs={{0,2},{1,3},{4,6},{5,7},{8,10},{9,11},{12,14},{13,15},{16,18},{17,... | collective-permute-start | bytes 6152 | tf_op jit(solution)/shard_map/ppermute | solution.py:236
  11.1 7.1 %collective-permute-start.1 = (s32[512]{0:T(512)S(1)}, s32[512]{0:T(512)S(1)}, u32[]{:S(2)}, u32[]{:S(2)}) collective-permute-start(s32[512]{0:T(512)S(1)} %bitcast.17), channel_id=1, source_target_pairs={{0,1},{1,2},{2,3},{4,5},{5,6},{6,7},{8,9},{9,10},{10,11},{12,13},{... | collective-permute-start | bytes 6152 | tf_op jit(solution)/shard_map/ppermute | solution.py:236
  18.7 7.3 %copy-start.12 = (s32[512]{0:T(512)}, s32[512]{0:T(512)S(1)}, u32[]{:S(2)}) copy-start(s32[512]{0:T(512)S(1)} %convert_reduce_fusion) | copy-start | bytes 6148
  36.7 62.2 %all-to-all-start.1 = ((bf16[32,16,2048]{2,1,0:T(8,128)(2,1)}), bf16[32,16,2048]{2,1,0:T(8,128)(2,1)}, u32[]{:S(2)}, u32[]{:S(2)}) async-start(bf16[32,16,2048]{2,1,0:T(8,128)(2,1)} %bitcast.10), calls=%async_computation.1 | async-start | bytes 4194304 | tf_op jit(solution)/shard_map/all_to_all | solution.py:190
  43.4 55.5 %copy-start.3 = (s32[1,512]{1,0:T(1,128)}, s32[1,512]{1,0:T(1,128)S(1)}, u32[]{:S(2)}) copy-start(s32[1,512]{1,0:T(1,128)S(1)} %get-tuple-element.19.place_ref) | copy-start | bytes 6148
  43.4 56.2 %copy-start.1 = (bf16[1024,512]{1,0:T(8,128)(2,1)}, bf16[1024,512]{1,0:T(8,128)(2,1)S(1)}, u32[]{:S(2)}) copy-start(bf16[1024,512]{1,0:T(8,128)(2,1)S(1)} %get-tuple-element.26.refs_9_) | copy-start | bytes 3145732
  43.4 55.5 %collective-permute-start.6 = (bf16[1024,512]{1,0:T(8,128)(2,1)S(1)}, bf16[1024,512]{1,0:T(8,128)(2,1)}, u32[]{:S(2)}, u32[]{:S(2)}) collective-permute-start(bf16[1024,512]{1,0:T(8,128)(2,1)S(1)} %get-tuple-element.26.refs_9_), channel_id=1, source_target_pairs={{0,1},{2,3},{4,5},{6,7},{8,9},{10,11},{12,13},{14,15},{16,17},{18,... | collective-permute-start | bytes 3145736 | tf_op jit(solution)/shard_map/ppermute | solution.py:278
  47.8 17.9 %collective-permute-start.5 = (bf16[256,512]{1,0:T(8,128)(2,1)S(1)}, bf16[256,512]{1,0:T(8,128)(2,1)S(1)}, u32[]{:S(2)}, u32[]{:S(2)}) collective-permute-start(bf16[256,512]{1,0:T(8,128)(2,1)S(1)} %get-tuple-element.25), channel_id=1, source_target_pairs={{0,2},{1,3},{4,6},{5,7},{8,10},{9,11},{12,14},{13,15},{16,18},{17,... | collective-permute-start | bytes 786440 | tf_op jit(solution)/shard_map/ppermute | solution.py:277
  49.1 25.5 %collective-permute-start.2 = (bf16[256,512]{1,0:T(8,128)(2,1)S(1)}, bf16[256,512]{1,0:T(8,128)(2,1)S(1)}, u32[]{:S(2)}, u32[]{:S(2)}) collective-permute-start(bf16[256,512]{1,0:T(8,128)(2,1)S(1)} %get-tuple-element.22), channel_id=1, source_target_pairs={{0,2},{1,3},{4,6},{5,7},{8,10},{9,11},{12,14},{13,15},{16,18},{17,... | collective-permute-start | bytes 786440 | tf_op jit(solution)/shard_map/ppermute | solution.py:277
  50.4 33.5 %collective-permute-start.3 = (bf16[256,512]{1,0:T(8,128)(2,1)S(1)}, bf16[256,512]{1,0:T(8,128)(2,1)S(1)}, u32[]{:S(2)}, u32[]{:S(2)}) collective-permute-start(bf16[256,512]{1,0:T(8,128)(2,1)S(1)} %get-tuple-element.23), channel_id=1, source_target_pairs={{0,2},{1,3},{4,6},{5,7},{8,10},{9,11},{12,14},{13,15},{16,18},{17,... | collective-permute-start | bytes 786440 | tf_op jit(solution)/shard_map/ppermute | solution.py:277
  51.7 37.7 %collective-permute-start.4 = (bf16[256,512]{1,0:T(8,128)(2,1)S(1)}, bf16[256,512]{1,0:T(8,128)(2,1)S(1)}, u32[]{:S(2)}, u32[]{:S(2)}) collective-permute-start(bf16[256,512]{1,0:T(8,128)(2,1)S(1)} %get-tuple-element.24), channel_id=1, source_target_pairs={{0,2},{1,3},{4,6},{5,7},{8,10},{9,11},{12,14},{13,15},{16,18},{17,... | collective-permute-start | bytes 786440 | tf_op jit(solution)/shard_map/ppermute | solution.py:277
  65.7 33.9 %copy-start.4 = (bf16[256,512]{1,0:T(8,128)(2,1)}, bf16[256,512]{1,0:T(8,128)(2,1)S(1)}, u32[]{:S(2)}) copy-start(bf16[256,512]{1,0:T(8,128)(2,1)S(1)} %collective-permute-done.5.refs_3_) | copy-start | bytes 786436
  65.7 25.0 %collective-permute-start.10 = (bf16[256,512]{1,0:T(8,128)(2,1)S(1)}, bf16[256,512]{1,0:T(8,128)(2,1)S(1)}, u32[]{:S(2)}, u32[]{:S(2)}) collective-permute-start(bf16[256,512]{1,0:T(8,128)(2,1)S(1)} %collective-permute-done.5.refs_3_), channel_id=1, source_target_pairs={{3,2},{7,6},{11,10},{15,14},{19,18},{23,22},{27,26},{31,30}} | collective-permute-start | bytes 786440 | tf_op jit(solution)/shard_map/ppermute | solution.py:279
  74.6 25.0 %copy-start.5 = (bf16[256,512]{1,0:T(8,128)(2,1)}, bf16[256,512]{1,0:T(8,128)(2,1)S(1)}, u32[]{:S(2)}) copy-start(bf16[256,512]{1,0:T(8,128)(2,1)S(1)} %collective-permute-done.2.refs_0_) | copy-start | bytes 786436
  74.6 16.1 %collective-permute-start.7 = (bf16[256,512]{1,0:T(8,128)(2,1)S(1)}, bf16[256,512]{1,0:T(8,128)(2,1)S(1)}, u32[]{:S(2)}, u32[]{:S(2)}) collective-permute-start(bf16[256,512]{1,0:T(8,128)(2,1)S(1)} %collective-permute-done.2.refs_0_), channel_id=1, source_target_pairs={{3,2},{7,6},{11,10},{15,14},{19,18},{23,22},{27,26},{31,30}} | collective-permute-start | bytes 786440 | tf_op jit(solution)/shard_map/ppermute | solution.py:279
  83.9 15.7 %copy-start.6 = (bf16[256,512]{1,0:T(8,128)(2,1)}, bf16[256,512]{1,0:T(8,128)(2,1)S(1)}, u32[]{:S(2)}) copy-start(bf16[256,512]{1,0:T(8,128)(2,1)S(1)} %collective-permute-done.3.refs_1_) | copy-start | bytes 786436
  83.9 9.4 %collective-permute-start.8 = (bf16[256,512]{1,0:T(8,128)(2,1)S(1)}, bf16[256,512]{1,0:T(8,128)(2,1)S(1)}, u32[]{:S(2)}, u32[]{:S(2)}) collective-permute-start(bf16[256,512]{1,0:T(8,128)(2,1)S(1)} %collective-permute-done.3.refs_1_), channel_id=1, source_target_pairs={{3,2},{7,6},{11,10},{15,14},{19,18},{23,22},{27,26},{31,30}} | collective-permute-start | bytes 786440 | tf_op jit(solution)/shard_map/ppermute | solution.py:279
  89.4 4.0 %copy-start.7 = (bf16[256,512]{1,0:T(8,128)(2,1)}, bf16[256,512]{1,0:T(8,128)(2,1)S(1)}, u32[]{:S(2)}) copy-start(bf16[256,512]{1,0:T(8,128)(2,1)S(1)} %collective-permute-done.4.refs_2_) | copy-start | bytes 786436
  89.4 9.5 %collective-permute-start.9 = (bf16[256,512]{1,0:T(8,128)(2,1)S(1)}, bf16[256,512]{1,0:T(8,128)(2,1)S(1)}, u32[]{:S(2)}, u32[]{:S(2)}) collective-permute-start(bf16[256,512]{1,0:T(8,128)(2,1)S(1)} %collective-permute-done.4.refs_2_), channel_id=1, source_target_pairs={{3,2},{7,6},{11,10},{15,14},{19,18},{23,22},{27,26},{31,30}} | collective-permute-start | bytes 786440 | tf_op jit(solution)/shard_map/ppermute | solution.py:279
  90.7 8.2 %copy-start.8 = (bf16[256,512]{1,0:T(8,128)(2,1)}, bf16[256,512]{1,0:T(8,128)(2,1)S(1)}, u32[]{:S(2)}) copy-start(bf16[256,512]{1,0:T(8,128)(2,1)S(1)} %collective-permute-done.10.refs_8_) | copy-start | bytes 786436
  90.7 8.2 %copy-start.9 = (bf16[256,512]{1,0:T(8,128)(2,1)}, bf16[256,512]{1,0:T(8,128)(2,1)S(1)}, u32[]{:S(2)}) copy-start(bf16[256,512]{1,0:T(8,128)(2,1)S(1)} %collective-permute-done.7.refs_5_) | copy-start | bytes 786436
  93.3 5.6 %copy-start.10 = (bf16[256,512]{1,0:T(8,128)(2,1)}, bf16[256,512]{1,0:T(8,128)(2,1)S(1)}, u32[]{:S(2)}) copy-start(bf16[256,512]{1,0:T(8,128)(2,1)S(1)} %collective-permute-done.8.refs_6_) | copy-start | bytes 786436
  98.9 0.7 copy-start.11
